TPU v7x, 128 devices: a whole 4x4x4 slice. The times are simulated.
128 devices in a mesh: gx: 8 (over y, core), gy: 16 (over x, z).
Axes of the slice: x: 4, y: 4, z: 4, core: 2. Of those that a mesh axis runs over, the one named last changes fastest.
Arguments:
- vectors: bfloat16 [32, 524288], P(None, ('gx', 'gy')), may hold values from -6 to 6
- near_tiles: bfloat16 [2048, 6, 256, 256], P(('gx', 'gy')), may hold values from -0.15625 to 0.15625
- near_list: int32 [2048, 6], P(('gx', 'gy')), may hold values from 0 to 2047, as said below
- leaf_basis: bfloat16 [2048, 64, 256], P(('gx', 'gy')), may hold values from -0.375 to 0.375
- leaf_transfer: bfloat16 [2048, 64, 64], P(('gx', 'gy')), may hold values from -0.1875 to 0.1875
- far_coupling: bfloat16 [2048, 24, 64, 64], P(('gx', 'gy')), may hold values from -0.15625 to 0.15625
- far_list: int32 [2048, 24], P(('gx', 'gy')), may hold values from 0 to 2047, as said below
- top_transfer: float32 [256, 64, 64], replicated, may hold values from -0.625 to 0.625
- top_coupling: float32 [256, 64, 64], replicated, may hold values from -0.75 to 0.75
Outputs:
- product: float32 [32, 524288], P(None, ('gx', 'gy'))
Inputs may be any that keep to these rules, and one draw needn't show every extreme that they name: `near_list`: entry 0 of a leaf's list is the leaf itself; the others are distinct leaves whose grid positions differ from the leaf's by at most one along each dimension. `far_list`: the entries of one leaf are distinct leaves whose parent boxes differ from the leaf's parent box by at most one along each dimension, and whose grid positions differ from the leaf's by two or more along some dimension.
All inputs are finite; a program needn't handle non-finite values.
Results may differ from a plain program's by a relative error of at most 0.0023.
Values may be sent and summed in bfloat16 or wider, within the bound.
A program may use at most 192 MiB of HBM per device.

v0:
```python
import jax
import jax.numpy as jnp
from jax import lax
from jax.experimental import pallas as pl
from jax.experimental.pallas import tpu as pltpu
from jax.sharding import PartitionSpec as P

LEAF = 256
R = 64
VEC = 32
LEAF_DEV = 16
NB = 6
K_FAR = 24
NDEV = 128
GX = 8
GY = 16
F32 = jnp.float32
BF16 = jnp.bfloat16
NT = (((1,), (1,)), ((), ()))
NN = (((1,), (0,)), ((), ()))
MESH = pl.DeviceIdType.MESH
PITCH = 256


def flip(value, bits):
    for k in range(3):
        bit = 1 << k
        if bits & bit:
            value = value + bit - 2 * bit * ((value // bit) % 2)
    return value


def dot(lhs, rhs, dims):
    return lax.dot_general(lhs, rhs, dims, preferred_element_type=F32)


def swap(block):
    return jnp.concatenate([block[:, R:], block[:, :R]], axis=1)


def low_lanes(rows):
    return lax.broadcasted_iota(jnp.int32, (rows, 2 * R), 1) < R


def split(block):
    high = block.astype(BF16)
    low = (block - high.astype(F32)).astype(BF16)
    return jnp.concatenate([high, low], axis=0)


def apply(block, pair):
    both = dot(split(block), jnp.concatenate([pair, pair], axis=0), NT)
    return both[:VEC] + both[VEC:]


def apply_transposed(block, pair):
    both = dot(split(block)[:, :R], pair, NN)
    both = both[:VEC] + both[VEC:]
    return both + swap(both)


def select_heap(top, lanes, found):
    row = lax.broadcasted_iota(jnp.int32, (16, 2 * NDEV), 0)
    lane = lax.broadcasted_iota(jnp.int32, (16, 2 * NDEV), 1)
    hot = jnp.zeros((16, 2 * NDEV), F32)
    for n, index in enumerate(lanes):
        hot = jnp.where((row == n) & (lane == index), 1.0, hot)
    hot = hot.astype(BF16)

    def one(r, _):
        picked = dot(hot, split(top[r]), NT)
        found[pl.ds(r, 16, stride=R), :] = picked
        return 0

    lax.fori_loop(0, R, one, 0, unroll=8)


def matrix(found, n):
    return found[n * R : (n + 1) * R, :].astype(BF16)


def kernel(
    vec_h, tiles_h, near_s, basis_h, lt_h, far_h, far_s, tt_h, tc_h, out,
    vec, tiles, basis, lt, far, tt, tc, xe, mp, me, found_t, found_c, trees, got, box,
    lsem, ssem, rsem,
):
    a = lax.axis_index("gx")
    b = lax.axis_index("gy")
    d = a * GY + b

    def local(n, source, target):
        return pltpu.make_async_copy(source, target, lsem.at[n])

    c_vec = local(0, vec_h, vec)
    c_basis = local(1, basis_h, basis)
    c_lt = local(2, lt_h, lt)
    c_tt = local(3, tt_h, tt)
    c_tc = local(4, tc_h, tc)
    c_tiles = [local(5 + n, tiles_h.at[pl.ds(4 * n, 4)], tiles.at[pl.ds(4 * n, 4)]) for n in range(4)]
    c_far = [local(9 + n, far_h.at[pl.ds(8 * n, 8)], far.at[pl.ds(8 * n, 8)]) for n in range(2)]
    for copy in [c_vec, c_basis, c_lt, c_tt, c_tc] + c_tiles + c_far:
        copy.start()

    gx_up = ((a + 1) % GX, b)
    gx_down = ((a + GX - 1) % GX, b)
    gy_up = (a, (b + 1) % GY)
    gy_down = (a, (b + GY - 1) % GY)
    x_of = b // 4
    z_of = b % 4
    group_a = [(a, x_of * 4 + flip(z_of, i)) for i in range(1, 4)]
    group_b = [(a, flip(x_of, i) * 4 + z_of) for i in range(1, 4)]
    group_c = [(flip(a, i), b) for i in range(1, 8)]
    partners = [gx_up, gx_down, gy_up, gy_down] + group_a + group_b + group_c
    barrier = pltpu.get_barrier_semaphore()
    for partner in partners:
        pl.semaphore_signal(barrier, inc=1, device_id=partner, device_id_type=MESH)

    def remote(n, source, target, partner):
        return pltpu.make_async_remote_copy(
            src_ref=source, dst_ref=target, send_sem=ssem.at[n], recv_sem=rsem.at[n],
            device_id=partner, device_id_type=MESH,
        )

    def leaves(start, count):
        return xe.at[pl.ds(start, count)]

    x_gy = []
    for n, x in enumerate((16, 32)):
        x_gy.append(remote(2 * n, leaves(x + 8, 4), leaves(x, 4), gy_up))
        x_gy.append(remote(2 * n + 1, leaves(x + 4, 4), leaves(x + 12, 4), gy_down))
    x_gx = [
        remote(4, leaves(36, 8), leaves(4, 8), gx_up),
        remote(5, leaves(20, 8), leaves(52, 8), gx_down),
    ]
    x_corner = []
    for n, y in enumerate((0, 12)):
        x_corner.append(remote(6 + 2 * n, leaves(32 + y, 4), leaves(y, 4), gx_up))
        x_corner.append(remote(7 + 2 * n, leaves(16 + y, 4), leaves(48 + y, 4), gx_down))
    m_gy = [remote(10, mp.at[4], mp.at[3], gy_up), remote(11, mp.at[4], mp.at[5], gy_down)]
    m_gx = [remote(12, mp.at[4], mp.at[1], gx_up), remote(13, mp.at[4], mp.at[7], gx_down)]
    m_corner = [
        remote(14, mp.at[3], mp.at[0], gx_up),
        remote(15, mp.at[3], mp.at[6], gx_down),
        remote(16, mp.at[5], mp.at[2], gx_up),
        remote(17, mp.at[5], mp.at[8], gx_down),
    ]
    t_a = [remote(17 + i, trees.at[0], got.at[i], group_a[i - 1]) for i in range(1, 4)]
    t_b = [remote(20 + i, trees.at[1], got.at[4 + i], group_b[i - 1]) for i in range(1, 4)]
    t_c = [remote(23 + i, trees.at[2], got.at[8 + i], group_c[i - 1]) for i in range(1, 8)]

    c_vec.wait()
    for m in range(LEAF_DEV):
        slot = (m % 2 + 1) * 16 + (m // 2 % 2 + 1) * 4 + m // 4
        xe[slot] = vec[:, m * LEAF : (m + 1) * LEAF]
    pl.semaphore_wait(barrier, len(partners))
    for copy in x_gy + x_gx:
        copy.start()

    low = low_lanes(VEC)
    c_basis.wait()
    for q in range(LEAF_DEV // 2):
        pair = jnp.concatenate(
            [vec[:, 2 * q * LEAF : (2 * q + 1) * LEAF], vec[:, (2 * q + 1) * LEAF : (2 * q + 2) * LEAF]], axis=0
        )
        weights = jnp.concatenate([basis[2 * q], basis[2 * q + 1]], axis=0)
        both = dot(pair, weights, NT)
        mp[4, q] = jnp.where(low, both[:VEC], both[VEC:]).astype(BF16)
    for copy in m_gy + m_gx:
        copy.start()

    c_lt.wait()
    box_0 = None
    for q in range(LEAF_DEV // 2):
        weights = jnp.concatenate([lt[2 * q], lt[2 * q + 1]], axis=1)
        term = dot(mp[4, q], jnp.concatenate([weights, weights], axis=0), NT)
        box_0 = term if box_0 is None else box_0 + term

    group = [d // 2**t for t in range(7)]

    def heap(t, g):
        return (NDEV >> t) + g

    c_tt.wait()
    select_heap(
        tt,
        [
            heap(0, group[0]), heap(1, group[1]), heap(1, flip(group[1], 1)), heap(2, group[2]), heap(3, group[3]),
            heap(3, flip(group[3], 1)), heap(4, group[4]), heap(5, group[5]), heap(5, flip(group[5], 2)),
            heap(5, flip(group[5], 3)),
        ],
        found_t,
    )
    trees[0] = jnp.where(low, box_0, apply(box_0, matrix(found_t, 0)))
    for copy in t_a:
        copy.start()
    c_tc.wait()
    select_heap(tc, [heap(t, group[t]) for t in range(7)], found_c)

    for copy in x_gy:
        copy.wait_recv()
    for copy in x_corner:
        copy.start()
    for copy in m_gy:
        copy.wait_recv()
    for copy in m_corner:
        copy.start()

    def first_of(block):
        return jnp.where(low, block, swap(block))

    def second_of(block):
        return jnp.where(low, swap(block), block)

    def climb(stage, copies, own_t, sibling_t):
        for copy in copies:
            copy.wait_recv()
        base = 4 * stage
        sibling = first_of(got[base + 1])
        own = second_of(trees[stage] + got[base + 1])
        other = second_of(got[base + 2] + got[base + 3])
        above = apply(own, matrix(found_t, own_t)) + apply(other, matrix(found_t, sibling_t))
        return sibling, other, above

    sib_0, sib_1, box_2 = climb(0, t_a, 1, 2)
    trees[1] = jnp.where(low, box_2, apply(box_2, matrix(found_t, 3)))
    for copy in t_b:
        copy.start()
    box[0] = apply(sib_0, matrix(found_c, 0))
    box[1] = apply(sib_1, matrix(found_c, 1))

    for copy in x_gx + x_corner:
        copy.wait_recv()

    x_base = 20 - 32 * a - 8 * b

    def near(l, _):
        total = None
        for j in range(NB):
            index = near_s[j, l]
            slot = 63 & (
                (index >> 8) * 32 + (index & 1) * 16 + ((index >> 4) & 15) * 8
                + (index & 2) * 2 + ((index >> 2) & 3) + x_base
            )
            term = dot(xe[slot], tiles[l, j], NT)
            total = term if total is None else total + term
        out[:, pl.ds(pl.multiple_of(l * LEAF, LEAF), LEAF)] = total
        return 0

    c_tiles[0].wait()
    c_tiles[1].wait()
    lax.fori_loop(0, 8, near, 0, unroll=4)

    sib_2, sib_3, box_4 = climb(1, t_b, 4, 5)
    trees[2] = jnp.where(low, box_4, apply(box_4, matrix(found_t, 6)))
    for copy in t_c:
        copy.start()
    box[2] = apply(sib_2, matrix(found_c, 2))
    box[3] = apply(sib_3, matrix(found_c, 3))

    c_tiles[2].wait()
    c_tiles[3].wait()
    lax.fori_loop(8, 16, near, 0, unroll=4)

    for copy in m_gx + m_corner:
        copy.wait_recv()

    def unpack(p, _):
        base = (p // 3) * PITCH + (p % 3) * LEAF_DEV
        for q in range(LEAF_DEV // 2):
            pair = mp[p, q]
            other = swap(pair)
            me[base + 2 * q] = jnp.where(low, pair, other)
            me[base + 2 * q + 1] = jnp.where(low, other, pair)
        return 0

    lax.fori_loop(0, 9, unpack, 0)

    for copy in t_c:
        copy.wait_recv()
    sib_4 = first_of(got[9])
    sib_5 = second_of(got[10] + got[11])
    sib_6 = apply(second_of(got[12] + got[13]), matrix(found_t, 8)) + apply(
        second_of(got[14] + got[15]), matrix(found_t, 9)
    )
    down = apply(sib_6, matrix(found_c, 6))
    down = apply(sib_5, matrix(found_c, 5)) + apply_transposed(down, matrix(found_t, 7))
    down = apply(sib_4, matrix(found_c, 4)) + apply_transposed(down, matrix(found_t, 6))
    down = box[3] + apply_transposed(down, matrix(found_t, 4))
    down = box[2] + apply_transposed(down, matrix(found_t, 3))
    down = box[1] + apply_transposed(down, matrix(found_t, 1))
    down = box[0] + apply_transposed(down, matrix(found_t, 0))
    local_box = split(down)[:, :R]

    for copy in c_far:
        copy.wait()
    m_base = (a - 1) * PITCH + (b - 1) * LEAF_DEV

    def finish(l, _):
        total = None
        for k in range(0, K_FAR, 4):
            moment = [me[(far_s[l, k + i] - m_base) & 1023] for i in range(4)]
            left = jnp.concatenate(
                [jnp.where(low, moment[0], moment[1]), jnp.where(low, moment[2], moment[3])], axis=1
            )
            right = jnp.concatenate([far[l, k + i] for i in range(4)], axis=1)
            term = dot(left, right, NT)
            total = term if total is None else total + term
        both = dot(local_box, lt[l], NN)
        coeffs = (total + (both[:VEC] + both[VEC:])).astype(BF16)
        at = pl.ds(pl.multiple_of(l * LEAF, LEAF), LEAF)
        out[:, at] = out[:, at] + dot(coeffs, basis[l], NN)
        return 0

    lax.fori_loop(0, LEAF_DEV, finish, 0, unroll=2)

    for copy in x_gy + x_gx + x_corner + m_gy + m_gx + m_corner + t_a + t_b + t_c:
        copy.wait_send()


def per_device(
    vectors, near_tiles, near_list, leaf_basis, leaf_transfer, far_coupling, far_list, top_transfer, top_coupling
):
    any_spec = pl.BlockSpec(memory_space=pl.ANY)
    smem = pl.BlockSpec(memory_space=pltpu.SMEM)
    return pl.pallas_call(
        kernel,
        out_shape=jax.ShapeDtypeStruct((VEC, LEAF_DEV * LEAF), F32),
        in_specs=[any_spec, any_spec, smem, any_spec, any_spec, any_spec, smem, any_spec, any_spec],
        out_specs=pl.BlockSpec(memory_space=pltpu.VMEM),
        scratch_shapes=[
            pltpu.VMEM((VEC, LEAF_DEV * LEAF), BF16),
            pltpu.VMEM((LEAF_DEV, NB, LEAF, LEAF), BF16),
            pltpu.VMEM((LEAF_DEV, R, LEAF), BF16),
            pltpu.VMEM((LEAF_DEV, R, R), BF16),
            pltpu.VMEM((LEAF_DEV, K_FAR, R, R), BF16),
            pltpu.VMEM((R, R, 2 * NDEV), F32),
            pltpu.VMEM((R, R, 2 * NDEV), F32),
            pltpu.VMEM((64, VEC, LEAF), BF16),
            pltpu.VMEM((9, LEAF_DEV // 2, VEC, 2 * R), BF16),
            pltpu.VMEM((1024, VEC, 2 * R), BF16),
            pltpu.VMEM((16 * R, 2 * R), F32),
            pltpu.VMEM((16 * R, 2 * R), F32),
            pltpu.VMEM((3, VEC, 2 * R), F32),
            pltpu.VMEM((16, VEC, 2 * R), F32),
            pltpu.VMEM((4, VEC, 2 * R), F32),
            pltpu.SemaphoreType.DMA((11,)),
            pltpu.SemaphoreType.DMA((31,)),
            pltpu.SemaphoreType.DMA((31,)),
        ],
        compiler_params=pltpu.CompilerParams(
            collective_id=0, has_side_effects=True, vmem_limit_bytes=56 << 20
        ),
        cost_estimate=pl.CostEstimate(flops=600_000_000, bytes_accessed=29_000_000, transcendentals=0),
    )(
        vectors,
        near_tiles,
        near_list.T,
        leaf_basis,
        leaf_transfer,
        far_coupling,
        far_list,
        jnp.transpose(top_transfer, (1, 2, 0)),
        jnp.transpose(top_coupling, (1, 2, 0)),
    )


def solution(mesh):
    placed = (
        P(None, ("gx", "gy")),
        P(("gx", "gy"), None, None, None),
        P(("gx", "gy"), None),
        P(("gx", "gy"), None, None),
        P(("gx", "gy"), None, None),
        P(("gx", "gy"), None, None, None),
        P(("gx", "gy"), None),
        P(),
        P(),
    )
    return jax.shard_map(
        per_device, mesh=mesh, in_specs=placed, out_specs=P(None, ("gx", "gy")), check_vma=False
    )
```

profile of v0, /device:TPU:1, one launch (start us, length us, event | category | flops | bytes accessed | tf_op | source)
XLA Modules:
  0.0 35.8 jit_solution(8918950367750929758)
XLA Ops:
  0.0 34.0 %shard_map.91 = f32[32,4096]{1,0:T(8,128)} custom-call(bf16[32,4096]{1,0:T(8,128)(2,1)} %vec_h.1, bf16[16,6,256,256]{3,2,1,0:T(8,128)(2,1)} %tiles_h.1, s32[6,16]{1,0:T(8,128)} %bitcast.5, bf16[16,64,256]{2,1,0:T(8,128)(2,1)} %basis_h.1, bf16[16,64,64]{2,1,0:T(8,128)(2,1)} %lt_h.1, bf16[16,24,64,64]{3,2,1,0:T(8,128)(2,1)} %far_h.1, s32[16,24]{1,0:T(8,128)} %far_s.1, ...), custom_call_target="tpu_custom_call" | custom-call | flops 600000000 | bytes 29000000 | tf_op jit(solution)/shard_map/pallas_call | solution.py:325
  34.0 1.9 %copy.11 = f32[32,4096]{1,0:T(8,128)} copy(f32[32,4096]{1,0:T(8,128)} %shard_map.91) | data formatting | bytes 1048576
where the time goes:
time: 36 us; the launch traced here: 35.8 us
  Pallas kernels  34 us (94%)
  local copies, waits for them, and re-layouts  1.87 us (5%)
    pallas_call x1, Pallas kernels, per_device(): pl.pallas_call(kernel, out_shape=jax.ShapeDtypeStruct((VEC, LEAF_DEV * LE...  34 us
    unnamed x1, local copies, waits for them, and re-layouts  1.87 us

commit v1 on v0

v1 whole, which is shorter than its diff:
```python
import jax
import jax.numpy as jnp
from jax import lax
from jax.experimental import pallas as pl
from jax.experimental.pallas import tpu as pltpu
from jax.sharding import PartitionSpec as P

LEAF = 256
R = 64
VEC = 32
LEAF_DEV = 16
NB = 6
K_FAR = 24
NDEV = 128
GX = 8
GY = 16
F32 = jnp.float32
BF16 = jnp.bfloat16
NT = (((1,), (1,)), ((), ()))
NN = (((1,), (0,)), ((), ()))
MESH = pl.DeviceIdType.MESH
PITCH = 256
PAIRS = LEAF_DEV // 2
HALF = VEC // 2


def flip(value, bits):
    for k in range(4):
        bit = 1 << k
        if bits & bit:
            value = value + bit - 2 * bit * ((value // bit) % 2)
    return value


def dot(lhs, rhs, dims):
    return lax.dot_general(lhs, rhs, dims, preferred_element_type=F32)


def swap(block):
    return jnp.concatenate([block[:, R:], block[:, :R]], axis=1)


def low_lanes(rows):
    return lax.broadcasted_iota(jnp.int32, (rows, 2 * R), 1) < R


def split(block):
    high = block.astype(BF16)
    low = (block - high.astype(F32)).astype(BF16)
    return jnp.concatenate([high, low], axis=0)


def apply(blocks, pairs):
    left = jnp.concatenate([split(block) for block in blocks], axis=1)
    right = jnp.concatenate([jnp.concatenate([pair, pair], axis=0) for pair in pairs], axis=1)
    both = dot(left, right, NT)
    rows = both.shape[0] // 2
    return both[:rows] + both[rows:]


def pair_of(block):
    high = block.astype(BF16)
    return jnp.where(low_lanes(R), high, (block - high.astype(F32)).astype(BF16))


def select_heap(top, lanes, found, rows):
    row = lax.broadcasted_iota(jnp.int32, (rows, 2 * NDEV), 0)
    lane = lax.broadcasted_iota(jnp.int32, (rows, 2 * NDEV), 1)
    wanted = jnp.full((rows, 2 * NDEV), -1, jnp.int32)
    for n, index in enumerate(lanes):
        wanted = jnp.where(row == n, index, wanted)
    hot = jnp.where(lane == wanted, 1.0, 0.0).astype(BF16)

    def one(r, _):
        found[pl.ds(r, rows, stride=R), :] = dot(hot, split(top[r]), NT)
        return 0

    lax.fori_loop(0, R, one, 0, unroll=16)


def matrix(found, n):
    return found[n * R : (n + 1) * R, :].astype(BF16)


def turned(found, n):
    block = found[n * R : (n + 1) * R, :].T
    return jnp.concatenate([block[:R], block[R:]], axis=1).astype(BF16)


def turned_whole(found, n):
    block = found[n * R : (n + 1) * R, :].T
    block = block[:R] + block[R:]
    return jnp.concatenate([block, block], axis=1)


def packed(block):
    return jnp.where(low_lanes(HALF), block[:HALF], block[HALF:])


def unpacked(block):
    low = low_lanes(HALF)
    other = swap(block)
    return jnp.concatenate([jnp.where(low, block, other), jnp.where(low, other, block)], axis=0)


def kernel(
    vec_h, tiles_h, near_s, basis_h, lt_h, far_h, far_s, tt_h, tc_h, out,
    vec, tiles, basis, lt, far, tt, tc, xe, mp, me, found_t, found_c, mine, got, got_top, near_sum, far_sum, tops,
    lsem, ssem, rsem,
):
    a = lax.axis_index("gx")
    b = lax.axis_index("gy")
    d = a * GY + b

    def local(n, source, target):
        return pltpu.make_async_copy(source, target, lsem.at[n])

    c_vec = local(0, vec_h, vec)
    c_basis = local(1, basis_h, basis)
    c_lt = local(2, lt_h, lt)
    c_tt = local(3, tt_h, tt)
    c_tc = local(4, tc_h, tc)
    c_own = local(5, tiles_h.at[:, pl.ds(0, 1)], tiles.at[:, pl.ds(0, 1)])
    c_far = local(6, far_h, far)
    c_tiles = local(7, tiles_h.at[:, pl.ds(1, NB - 1)], tiles.at[:, pl.ds(1, NB - 1)])
    ALL = [c_vec, c_basis, c_lt, c_tt, c_tc, c_own, c_far, c_tiles]
    for copy in ALL[:3]:
        copy.start()

    gx_up = ((a + 1) % GX, b)
    gx_down = ((a + GX - 1) % GX, b)
    gy_up = (a, (b + 1) % GY)
    gy_down = (a, (b + GY - 1) % GY)
    group_y = [(a, flip(b, i)) for i in range(1, GY)]
    group_x = [(flip(a, i), b) for i in range(1, GX)]
    barrier = pltpu.get_barrier_semaphore()
    for partner in group_y + group_x:
        pl.semaphore_signal(barrier, inc=1, device_id=partner, device_id_type=MESH)

    def remote(n, source, target, partner):
        return pltpu.make_async_remote_copy(
            src_ref=source, dst_ref=target, send_sem=ssem.at[n], recv_sem=rsem.at[n],
            device_id=partner, device_id_type=MESH,
        )

    def leaves(start, count):
        return xe.at[pl.ds(start, count)]

    x_gy = []
    for n, x in enumerate((16, 32)):
        x_gy.append(remote(2 * n, leaves(x + 8, 4), leaves(x, 4), gy_up))
        x_gy.append(remote(2 * n + 1, leaves(x + 4, 4), leaves(x + 12, 4), gy_down))
    x_gx = [
        remote(4, leaves(36, 8), leaves(4, 8), gx_up),
        remote(5, leaves(20, 8), leaves(52, 8), gx_down),
    ]
    x_corner = []
    for n, y in enumerate((0, 12)):
        x_corner.append(remote(6 + 2 * n, leaves(32 + y, 4), leaves(y, 4), gx_up))
        x_corner.append(remote(7 + 2 * n, leaves(16 + y, 4), leaves(48 + y, 4), gx_down))
    m_gy = [remote(10, mp.at[4], mp.at[3], gy_up), remote(11, mp.at[4], mp.at[5], gy_down)]
    m_gx = [remote(12, mp.at[4], mp.at[1], gx_up), remote(13, mp.at[4], mp.at[7], gx_down)]
    m_corner = [
        remote(14, mp.at[3], mp.at[0], gx_up),
        remote(15, mp.at[3], mp.at[6], gx_down),
        remote(16, mp.at[5], mp.at[2], gx_up),
        remote(17, mp.at[5], mp.at[8], gx_down),
    ]
    t_low = [remote(17 + i, mine.at[0], got.at[i], group_y[i - 1]) for i in range(1, GY)]
    t_top = [remote(32 + i, mine.at[1 if i == 1 else 2], got_top.at[i], group_x[i - 1]) for i in range(1, GX)]

    low = low_lanes(VEC)
    c_vec.wait()
    for m in range(LEAF_DEV):
        slot = (m % 2 + 1) * 16 + (m // 2 % 2 + 1) * 4 + m // 4
        xe[slot] = vec[:, m * LEAF : (m + 1) * LEAF]
    pl.semaphore_wait(barrier, len(group_y) + len(group_x))
    for copy in x_gy + x_gx:
        copy.start()
    c_basis.wait()
    c_lt.wait()
    for copy in ALL[3:]:
        copy.start()
    for q in range(PAIRS):
        pair = jnp.concatenate(
            [vec[:, 2 * q * LEAF : (2 * q + 1) * LEAF], vec[:, (2 * q + 1) * LEAF : (2 * q + 2) * LEAF]], axis=0
        )
        weights = jnp.concatenate([basis[2 * q], basis[2 * q + 1]], axis=0)
        both = dot(pair, weights, NT)
        mp[4, q] = jnp.where(low, both[:VEC], both[VEC:]).astype(BF16)
    box_0 = None
    for q in range(PAIRS):
        weights = jnp.concatenate([lt[2 * q], lt[2 * q + 1]], axis=1)
        term = dot(mp[4, q], jnp.concatenate([weights, weights], axis=0), NT)
        box_0 = term if box_0 is None else box_0 + term
    mine[0] = packed(box_0)
    for copy in t_low + m_gy + m_gx:
        copy.start()

    group = [d // 2**t for t in range(7)]

    def heap(t, flipped=0):
        return (NDEV >> t) + flip(group[t], flipped)

    lanes = [heap(0, i) for i in range(16)] + [heap(1, i) for i in range(8)] + [heap(2, i) for i in range(4)]
    lanes += [heap(3), heap(3, 1), heap(4), heap(5), heap(5, 2), heap(5, 3)]
    first = {0: 0, 1: 16, 2: 24, 3: 28, 4: 30, 5: 31}
    c_tt.wait()
    select_heap(tt, lanes, found_t, 48)
    c_tc.wait()
    select_heap(tc, [heap(t) for t in range(7)], found_c, 16)

    def unpack(p):
        base = (p // 3) * PITCH + (p % 3) * LEAF_DEV
        for q in range(PAIRS):
            pair = mp[p, q]
            other = swap(pair)
            me[base + 2 * q] = jnp.where(low, pair, other)
            me[base + 2 * q + 1] = jnp.where(low, other, pair)

    for copy in x_gy:
        copy.wait_recv()
    for copy in x_corner:
        copy.start()
    for copy in m_gy:
        copy.wait_recv()
    for copy in m_corner:
        copy.start()
    unpack(4)
    c_own.wait()
    for m in range(LEAF_DEV):
        near_sum[m] = dot(vec[:, m * LEAF : (m + 1) * LEAF], tiles[m, 0], NT)

    for copy in t_low:
        copy.wait_recv()
    boxes = [box_0] + [unpacked(got[i]) for i in range(1, GY)]
    siblings = []
    for t in range(4):
        siblings.append(boxes[1])
        boxes = [
            apply(
                [boxes[2 * j], boxes[2 * j + 1]],
                [matrix(found_t, first[t] + 2 * j), matrix(found_t, first[t] + 2 * j + 1)],
            )
            for j in range(len(boxes) // 2)
        ]
    mine[1] = packed(boxes[0])
    mine[2] = packed(apply(boxes, [matrix(found_t, first[4])]))
    for copy in t_top:
        copy.start()
    down = apply([siblings[3]], [matrix(found_c, 3)])
    for t in (2, 1, 0):
        down = apply([siblings[t], down], [matrix(found_c, t), turned(found_t, first[t])])

    chain = turned_whole(found_t, first[0])
    for t in (1, 2, 3):
        chain = apply([chain], [matrix(found_t, first[t])])
    top_weights = [pair_of(apply([chain], [turned(found_c, 4)]))]
    chain = apply([chain], [matrix(found_t, first[4])])
    top_weights.append(pair_of(apply([chain], [turned(found_c, 5)])))
    chain = apply([chain], [matrix(found_t, first[5])])
    chain = apply([chain], [turned(found_c, 6)])
    for n in (1, 2):
        top_weights.append(pair_of(apply([chain], [turned(found_t, first[5] + n)])))
    for n in range(4):
        tops[n] = top_weights[n]

    unpack(3)
    unpack(5)
    for copy in m_gx:
        copy.wait_recv()
    unpack(1)
    unpack(7)
    for copy in x_gx + x_corner:
        copy.wait_recv()
    c_tiles.wait()
    x_base = 20 - 32 * a - 8 * b

    def near_leaf(l, _):
        total = near_sum[l]
        for j in range(1, NB):
            index = near_s[j, l]
            slot = 63 & (
                (index >> 8) * 32 + (index & 1) * 16 + ((index >> 4) & 15) * 8
                + (index & 2) * 2 + ((index >> 2) & 3) + x_base
            )
            total = total + dot(xe[slot], tiles[l, j], NT)
        near_sum[l] = total
        return 0

    lax.fori_loop(0, LEAF_DEV, near_leaf, 0, unroll=16)

    for copy in m_corner:
        copy.wait_recv()
    for p in (0, 2, 6, 8):
        unpack(p)
    c_far.wait()
    m_base = (a - 1) * PITCH + (b - 1) * LEAF_DEV

    def far_leaf(l, _):
        total = None
        for k in range(0, K_FAR, 4):
            moment = [me[(far_s[l, k + i] - m_base) & 1023] for i in range(4)]
            left = jnp.concatenate(
                [jnp.where(low, moment[0], moment[1]), jnp.where(low, moment[2], moment[3])], axis=1
            )
            right = jnp.concatenate([far[l, k + i] for i in range(4)], axis=1)
            term = dot(left, right, NT)
            total = term if total is None else total + term
        far_sum[l] = total
        return 0

    lax.fori_loop(0, LEAF_DEV, far_leaf, 0, unroll=8)

    for copy in t_top:
        copy.wait_recv()
    top = [None] + [unpacked(got_top[i]) for i in range(1, GX)]
    down = down + apply([top[1], top[2] + top[3], top[4] + top[5], top[6] + top[7]], [tops[n] for n in range(4)])
    high = down.astype(BF16)
    rest = (down - high.astype(F32)).astype(BF16)
    local_box = jnp.where(low, high, rest)
    for m in range(LEAF_DEV):
        from_box = dot(local_box, jnp.concatenate([lt[m], lt[m]], axis=0), NN)
        coeffs = (far_sum[m] + from_box).astype(BF16)
        out[:, m * LEAF : (m + 1) * LEAF] = near_sum[m] + dot(coeffs, basis[m], NN)

    for copy in x_gy + x_gx + x_corner + m_gy + m_gx + m_corner + t_low + t_top:
        copy.wait_send()


def per_device(
    vectors, near_tiles, near_list, leaf_basis, leaf_transfer, far_coupling, far_list, top_transfer, top_coupling
):
    any_spec = pl.BlockSpec(memory_space=pltpu.HBM)
    smem = pl.BlockSpec(memory_space=pltpu.SMEM)
    return pl.pallas_call(
        kernel,
        out_shape=pltpu.VMEM((VEC, LEAF_DEV * LEAF), F32),
        in_specs=[any_spec, any_spec, smem, any_spec, any_spec, any_spec, smem, any_spec, any_spec],
        out_specs=pl.BlockSpec(memory_space=pltpu.VMEM),
        scratch_shapes=[
            pltpu.VMEM((VEC, LEAF_DEV * LEAF), BF16),
            pltpu.VMEM((LEAF_DEV, NB, LEAF, LEAF), BF16),
            pltpu.VMEM((LEAF_DEV, R, LEAF), BF16),
            pltpu.VMEM((LEAF_DEV, R, R), BF16),
            pltpu.VMEM((LEAF_DEV, K_FAR, R, R), BF16),
            pltpu.VMEM((R, R, 2 * NDEV), F32),
            pltpu.VMEM((R, R, 2 * NDEV), F32),
            pltpu.VMEM((64, VEC, LEAF), BF16),
            pltpu.VMEM((9, PAIRS, VEC, 2 * R), BF16),
            pltpu.VMEM((1024, VEC, 2 * R), BF16),
            pltpu.VMEM((48 * R, 2 * R), F32),
            pltpu.VMEM((16 * R, 2 * R), F32),
            pltpu.VMEM((3, HALF, 2 * R), F32),
            pltpu.VMEM((GY, HALF, 2 * R), F32),
            pltpu.VMEM((GX, HALF, 2 * R), F32),
            pltpu.VMEM((LEAF_DEV, VEC, LEAF), F32),
            pltpu.VMEM((LEAF_DEV, VEC, R), F32),
            pltpu.VMEM((4, R, 2 * R), BF16),
            pltpu.SemaphoreType.DMA((8,)),
            pltpu.SemaphoreType.DMA((40,)),
            pltpu.SemaphoreType.DMA((40,)),
        ],
        compiler_params=pltpu.CompilerParams(
            collective_id=0, has_side_effects=True, vmem_limit_bytes=60 << 20
        ),
        cost_estimate=pl.CostEstimate(flops=600_000_000, bytes_accessed=29_000_000, transcendentals=0),
    )(
        vectors,
        near_tiles,
        near_list.T,
        leaf_basis,
        leaf_transfer,
        far_coupling,
        far_list,
        jnp.transpose(top_transfer, (1, 2, 0)),
        jnp.transpose(top_coupling, (1, 2, 0)),
    )


def solution(mesh):
    placed = (
        P(None, ("gx", "gy")),
        P(("gx", "gy"), None, None, None),
        P(("gx", "gy"), None),
        P(("gx", "gy"), None, None),
        P(("gx", "gy"), None, None),
        P(("gx", "gy"), None, None, None),
        P(("gx", "gy"), None),
        P(),
        P(),
    )
    return jax.shard_map(
        per_device, mesh=mesh, in_specs=placed, out_specs=P(None, ("gx", "gy")), check_vma=False
    )
```

time: 36 us -> 29.5 us (0.82)
  Pallas kernels: 34 us -> 28.5 us
  local copies, waits for them, and re-layouts: 1.87 us -> 0.8 us
    pallas_call x1, Pallas kernels: 34 us -> 28.5 us  [per_device(): pl.pallas_call(kernel, out_shape=pltpu.VMEM((VEC, LEAF_DEV * LEAF), F32),...]
    unnamed x1, local copies, waits for them, and re-layouts: 1.87 us -> 0.8 us
where the time goes in v1:
time: 29.5 us; the launch traced here: 29.3 us
  Pallas kernels  28.5 us (97%)
  local copies, waits for them, and re-layouts  0.8 us (3%)
    pallas_call x1, Pallas kernels, per_device(): pl.pallas_call(kernel, out_shape=pltpu.VMEM((VEC, LEAF_DEV * LEAF), F32),...  28.5 us
    unnamed x1, local copies, waits for them, and re-layouts  0.8 us

profile of v1, /device:TPU:1, one launch (start us, length us, event | category | flops | bytes accessed | tf_op | source)
XLA Modules:
  0.0 29.3 jit_solution(11008507631557384434)
XLA Ops:
  0.0 28.5 %shard_map.91 = f32[32,4096]{1,0:T(8,128)S(1)} custom-call(bf16[32,4096]{1,0:T(8,128)(2,1)} %vec_h.1, bf16[16,6,256,256]{3,2,1,0:T(8,128)(2,1)} %tiles_h.1, s32[6,16]{1,0:T(8,128)} %bitcast.5, bf16[16,64,256]{2,1,0:T(8,128)(2,1)} %basis_h.1, bf16[16,64,64]{2,1,0:T(8,128)(2,1)} %lt_h.1, bf16[16,24,64,64]{3,2,1,0:T(8,128)(2,1)} %far_h.1, s32[16,24]{1,0:T(8,128)} %far_s.1, ...), custom_call_target="tpu_custom_call" | custom-call | flops 600000000 | bytes 29000000 | tf_op jit(solution)/shard_map/pallas_call | solution.py:336
  28.5 0.8 %copy.11 = f32[32,4096]{1,0:T(8,128)} copy(f32[32,4096]{1,0:T(8,128)S(1)} %shard_map.91) | data formatting | bytes 1048576

commit v2 on v1

--- a/solution.py
+++ b/solution.py
@@ -105,7 +105,7 @@
 
 def kernel(
     vec_h, tiles_h, near_s, basis_h, lt_h, far_h, far_s, tt_h, tc_h, out,
-    vec, tiles, basis, lt, far, tt, tc, xe, mp, me, found_t, found_c, mine, got, got_top, near_sum, far_sum, tops,
+    vec, tiles, basis, lt, far, tt, tc, xn, xf, mp, me, found_t, found_c, mine, got, got_top, near_sum, far_sum, tops,
     lsem, ssem, rsem,
 ):
     a = lax.axis_index("gx")
@@ -123,7 +123,7 @@
     c_own = local(5, tiles_h.at[:, pl.ds(0, 1)], tiles.at[:, pl.ds(0, 1)])
     c_far = local(6, far_h, far)
     c_tiles = local(7, tiles_h.at[:, pl.ds(1, NB - 1)], tiles.at[:, pl.ds(1, NB - 1)])
-    ALL = [c_vec, c_basis, c_lt, c_tt, c_tc, c_own, c_far, c_tiles]
+    ALL = [c_vec, c_basis, c_lt, c_tt, c_tc, c_own, c_tiles, c_far]
     for copy in ALL[:3]:
         copy.start()
 
@@ -143,21 +143,22 @@
             device_id=partner, device_id_type=MESH,
         )
 
-    def leaves(start, count):
-        return xe.at[pl.ds(start, count)]
-
-    x_gy = []
-    for n, x in enumerate((16, 32)):
-        x_gy.append(remote(2 * n, leaves(x + 8, 4), leaves(x, 4), gy_up))
-        x_gy.append(remote(2 * n + 1, leaves(x + 4, 4), leaves(x + 12, 4), gy_down))
-    x_gx = [
-        remote(4, leaves(36, 8), leaves(4, 8), gx_up),
-        remote(5, leaves(20, 8), leaves(52, 8), gx_down),
+    core = a % 2
+    chip = (flip(a, 1), b)
+    off = ((a + 2 * core + GX - 1) % GX, b)
+
+    def move(n, ref, source, target, count, partner):
+        return remote(n, ref.at[pl.ds(source, count)], ref.at[pl.ds(target, count)], partner)
+
+    x_gy = [
+        move(0, xf, 24, 16, 4, gy_up), move(1, xf, 20, 28, 4, gy_down),
+        move(2, xn, 24, 16, 4, gy_up), move(3, xn, 20, 28, 4, gy_down),
     ]
-    x_corner = []
-    for n, y in enumerate((0, 12)):
-        x_corner.append(remote(6 + 2 * n, leaves(32 + y, 4), leaves(y, 4), gx_up))
-        x_corner.append(remote(7 + 2 * n, leaves(16 + y, 4), leaves(48 + y, 4), gx_down))
+    x_gx = [move(4, xf, 20, 36, 8, off), move(5, xn, 20, 36, 8, chip)]
+    x_corner = [
+        move(6, xf, 16, 32, 4, off), move(7, xf, 28, 44, 4, off),
+        move(8, xn, 16, 32, 4, chip), move(9, xn, 28, 44, 4, chip),
+    ]
     m_gy = [remote(10, mp.at[4], mp.at[3], gy_up), remote(11, mp.at[4], mp.at[5], gy_down)]
     m_gx = [remote(12, mp.at[4], mp.at[1], gx_up), remote(13, mp.at[4], mp.at[7], gx_down)]
     m_corner = [
@@ -172,11 +173,11 @@
     low = low_lanes(VEC)
     c_vec.wait()
     for m in range(LEAF_DEV):
-        slot = (m % 2 + 1) * 16 + (m // 2 % 2 + 1) * 4 + m // 4
-        xe[slot] = vec[:, m * LEAF : (m + 1) * LEAF]
-    pl.semaphore_wait(barrier, len(group_y) + len(group_x))
-    for copy in x_gy + x_gx:
-        copy.start()
+        place = (m // 2 % 2 + 1) * 4 + m // 4
+        beside = 1 - core if m % 2 else core
+        block = vec[:, m * LEAF : (m + 1) * LEAF]
+        xn[beside * 16 + place] = block
+        xf[(1 - beside) * 16 + place] = block
     c_basis.wait()
     c_lt.wait()
     for copy in ALL[3:]:
@@ -194,7 +195,8 @@
         term = dot(mp[4, q], jnp.concatenate([weights, weights], axis=0), NT)
         box_0 = term if box_0 is None else box_0 + term
     mine[0] = packed(box_0)
-    for copy in t_low + m_gy + m_gx:
+    pl.semaphore_wait(barrier, len(group_y) + len(group_x))
+    for copy in t_low[::-1] + x_gy + m_gy + x_gx + m_gx:
         copy.start()
 
     group = [d // 2**t for t in range(7)]
@@ -218,19 +220,32 @@
             me[base + 2 * q] = jnp.where(low, pair, other)
             me[base + 2 * q + 1] = jnp.where(low, other, pair)
 
-    for copy in x_gy:
-        copy.wait_recv()
-    for copy in x_corner:
-        copy.start()
-    for copy in m_gy:
-        copy.wait_recv()
-    for copy in m_corner:
-        copy.start()
     unpack(4)
     c_own.wait()
     for m in range(LEAF_DEV):
         near_sum[m] = dot(vec[:, m * LEAF : (m + 1) * LEAF], tiles[m, 0], NT)
 
+    chain = turned_whole(found_t, first[0])
+    for t in (1, 2, 3):
+        chain = apply([chain], [matrix(found_t, first[t])])
+    top_weights = [pair_of(apply([chain], [turned(found_c, 4)]))]
+    chain = apply([chain], [matrix(found_t, first[4])])
+    top_weights.append(pair_of(apply([chain], [turned(found_c, 5)])))
+    chain = apply([chain], [matrix(found_t, first[5])])
+    chain = apply([chain], [turned(found_c, 6)])
+    for n in (1, 2):
+        top_weights.append(pair_of(apply([chain], [turned(found_t, first[5] + n)])))
+    for n in range(4):
+        tops[n] = top_weights[n]
+
+    for copy in x_gy:
+        copy.wait_recv()
+    for copy in x_corner:
+        copy.start()
+    for slot in (0, 12):
+        for z in range(4):
+            xn[slot + z] = xf[16 + slot + z]
+            xf[slot + z] = xn[16 + slot + z]
     for copy in t_low:
         copy.wait_recv()
     boxes = [box_0] + [unpacked(got[i]) for i in range(1, GY)]
@@ -246,49 +261,45 @@
         ]
     mine[1] = packed(boxes[0])
     mine[2] = packed(apply(boxes, [matrix(found_t, first[4])]))
-    for copy in t_top:
-        copy.start()
+    for copy in reversed(t_top):
+        copy.start()
+    for copy in m_gy:
+        copy.wait_recv()
+    for copy in m_corner:
+        copy.start()
+    def near_side(ref, copies, column, turn, base):
+        for copy in copies:
+            copy.wait_recv()
+        base = base * 16 + turn * (16 - 32 * a) + 4 - 8 * b
+
+        def near_leaf(i, _):
+            m = column + 2 * i
+            total = near_sum[m]
+            for j in range(1, NB):
+                index = near_s[j, m]
+                slot = 63 & (
+                    turn * ((index >> 8) * 32 + (index & 1) * 16) + ((index >> 4) & 15) * 8
+                    + (index & 2) * 2 + ((index >> 2) & 3) + base
+                )
+                total = total + dot(ref[slot], tiles[m, j], NT)
+            near_sum[m] = total
+            return 0
+
+        lax.fori_loop(0, PAIRS, near_leaf, 0, unroll=8)
+
+    c_tiles.wait()
+    near_side(xn, [x_gx[1]] + x_corner[2:], 1 - core, 1 - 2 * core, 3 * core - 1)
     down = apply([siblings[3]], [matrix(found_c, 3)])
     for t in (2, 1, 0):
         down = apply([siblings[t], down], [matrix(found_c, t), turned(found_t, first[t])])
 
-    chain = turned_whole(found_t, first[0])
-    for t in (1, 2, 3):
-        chain = apply([chain], [matrix(found_t, first[t])])
-    top_weights = [pair_of(apply([chain], [turned(found_c, 4)]))]
-    chain = apply([chain], [matrix(found_t, first[4])])
-    top_weights.append(pair_of(apply([chain], [turned(found_c, 5)])))
-    chain = apply([chain], [matrix(found_t, first[5])])
-    chain = apply([chain], [turned(found_c, 6)])
-    for n in (1, 2):
-        top_weights.append(pair_of(apply([chain], [turned(found_t, first[5] + n)])))
-    for n in range(4):
-        tops[n] = top_weights[n]
-
     unpack(3)
     unpack(5)
     for copy in m_gx:
         copy.wait_recv()
     unpack(1)
     unpack(7)
-    for copy in x_gx + x_corner:
-        copy.wait_recv()
-    c_tiles.wait()
-    x_base = 20 - 32 * a - 8 * b
-
-    def near_leaf(l, _):
-        total = near_sum[l]
-        for j in range(1, NB):
-            index = near_s[j, l]
-            slot = 63 & (
-                (index >> 8) * 32 + (index & 1) * 16 + ((index >> 4) & 15) * 8
-                + (index & 2) * 2 + ((index >> 2) & 3) + x_base
-            )
-            total = total + dot(xe[slot], tiles[l, j], NT)
-        near_sum[l] = total
-        return 0
-
-    lax.fori_loop(0, LEAF_DEV, near_leaf, 0, unroll=16)
+    near_side(xf, [x_gx[0]] + x_corner[:2], core, 2 * core - 1, 2 - 3 * core)
 
     for copy in m_corner:
         copy.wait_recv()
@@ -346,6 +357,7 @@
             pltpu.VMEM((LEAF_DEV, K_FAR, R, R), BF16),
             pltpu.VMEM((R, R, 2 * NDEV), F32),
             pltpu.VMEM((R, R, 2 * NDEV), F32),
+            pltpu.VMEM((64, VEC, LEAF), BF16),
             pltpu.VMEM((64, VEC, LEAF), BF16),
             pltpu.VMEM((9, PAIRS, VEC, 2 * R), BF16),
             pltpu.VMEM((1024, VEC, 2 * R), BF16),

time: 29.5 us -> 28.2 us (0.956)
  Pallas kernels: 28.5 us -> 27.2 us
    pallas_call x1, Pallas kernels: 28.5 us -> 27.2 us  [per_device(): pl.pallas_call(kernel, out_shape=pltpu.VMEM((VEC, LEAF_DEV * LEAF), F32),...]
where the time goes in v2:
time: 28.2 us; the launch traced here: 28 us
  Pallas kernels  27.2 us (96%)
  local copies, waits for them, and re-layouts  0.8 us (3%)
    pallas_call x1, Pallas kernels, per_device(): pl.pallas_call(kernel, out_shape=pltpu.VMEM((VEC, LEAF_DEV * LEAF), F32),...  27.2 us
    unnamed x1, local copies, waits for them, and re-layouts  0.8 us

profile of v2, /device:TPU:1, one launch (start us, length us, event | category | flops | bytes accessed | tf_op | source)
XLA Modules:
  0.0 28.0 jit_solution(18103024768965706794)
XLA Ops:
  0.0 27.2 %shard_map.91 = f32[32,4096]{1,0:T(8,128)S(1)} custom-call(bf16[32,4096]{1,0:T(8,128)(2,1)} %vec_h.1, bf16[16,6,256,256]{3,2,1,0:T(8,128)(2,1)} %tiles_h.1, s32[6,16]{1,0:T(8,128)} %bitcast.5, bf16[16,64,256]{2,1,0:T(8,128)(2,1)} %basis_h.1, bf16[16,64,64]{2,1,0:T(8,128)(2,1)} %lt_h.1, bf16[16,24,64,64]{3,2,1,0:T(8,128)(2,1)} %far_h.1, s32[16,24]{1,0:T(8,128)} %far_s.1, ...), custom_call_target="tpu_custom_call" | custom-call | flops 600000000 | bytes 29000000 | tf_op jit(solution)/shard_map/pallas_call | solution.py:347
  27.2 0.8 %copy.11 = f32[32,4096]{1,0:T(8,128)} copy(f32[32,4096]{1,0:T(8,128)S(1)} %shard_map.91) | data formatting | bytes 1048576

commit v3 on v2

--- a/solution.py
+++ b/solution.py
@@ -104,8 +104,8 @@
 
 
 def kernel(
-    vec_h, tiles_h, near_s, basis_h, lt_h, far_h, far_s, tt_h, tc_h, out,
-    vec, tiles, basis, lt, far, tt, tc, xn, xf, mp, me, found_t, found_c, mine, got, got_top, near_sum, far_sum, tops,
+    vec_h, tiles_h, near_h, basis_h, lt_h, far_h, list_h, tt_h, tc_h, out,
+    vec, tiles, basis, lt, far, tt, tc, xn, xf, mp, me, found_t, found_c, mine, got, got_top, near_sum, far_sum, tops, near_s, far_s,
     lsem, ssem, rsem,
 ):
     a = lax.axis_index("gx")
@@ -123,7 +123,9 @@
     c_own = local(5, tiles_h.at[:, pl.ds(0, 1)], tiles.at[:, pl.ds(0, 1)])
     c_far = local(6, far_h, far)
     c_tiles = local(7, tiles_h.at[:, pl.ds(1, NB - 1)], tiles.at[:, pl.ds(1, NB - 1)])
-    ALL = [c_vec, c_basis, c_lt, c_tt, c_tc, c_own, c_tiles, c_far]
+    c_near_list = local(8, near_h, near_s)
+    c_far_list = local(9, list_h, far_s)
+    ALL = [c_vec, c_basis, c_lt, c_tt, c_tc, c_own, c_tiles, c_far, c_near_list, c_far_list]
     for copy in ALL[:3]:
         copy.start()
 
@@ -288,6 +290,8 @@
         lax.fori_loop(0, PAIRS, near_leaf, 0, unroll=8)
 
     c_tiles.wait()
+    c_near_list.wait()
+    c_far_list.wait()
     near_side(xn, [x_gx[1]] + x_corner[2:], 1 - core, 1 - 2 * core, 3 * core - 1)
     down = apply([siblings[3]], [matrix(found_c, 3)])
     for t in (2, 1, 0):
@@ -299,6 +303,8 @@
         copy.wait_recv()
     unpack(1)
     unpack(7)
+    for copy in x_gy + x_gx + m_gy + m_gx + t_low:
+        copy.wait_send()
     near_side(xf, [x_gx[0]] + x_corner[:2], core, 2 * core - 1, 2 - 3 * core)
 
     for copy in m_corner:
@@ -335,7 +341,7 @@
         coeffs = (far_sum[m] + from_box).astype(BF16)
         out[:, m * LEAF : (m + 1) * LEAF] = near_sum[m] + dot(coeffs, basis[m], NN)
 
-    for copy in x_gy + x_gx + x_corner + m_gy + m_gx + m_corner + t_low + t_top:
+    for copy in x_corner + m_corner + t_top:
         copy.wait_send()
 
 
@@ -343,11 +349,10 @@
     vectors, near_tiles, near_list, leaf_basis, leaf_transfer, far_coupling, far_list, top_transfer, top_coupling
 ):
     any_spec = pl.BlockSpec(memory_space=pltpu.HBM)
-    smem = pl.BlockSpec(memory_space=pltpu.SMEM)
     return pl.pallas_call(
         kernel,
         out_shape=pltpu.VMEM((VEC, LEAF_DEV * LEAF), F32),
-        in_specs=[any_spec, any_spec, smem, any_spec, any_spec, any_spec, smem, any_spec, any_spec],
+        in_specs=[any_spec] * 9,
         out_specs=pl.BlockSpec(memory_space=pltpu.VMEM),
         scratch_shapes=[
             pltpu.VMEM((VEC, LEAF_DEV * LEAF), BF16),
@@ -369,7 +374,9 @@
             pltpu.VMEM((LEAF_DEV, VEC, LEAF), F32),
             pltpu.VMEM((LEAF_DEV, VEC, R), F32),
             pltpu.VMEM((4, R, 2 * R), BF16),
-            pltpu.SemaphoreType.DMA((8,)),
+            pltpu.SMEM((NB, LEAF_DEV), jnp.int32),
+            pltpu.SMEM((LEAF_DEV, K_FAR), jnp.int32),
+            pltpu.SemaphoreType.DMA((10,)),
             pltpu.SemaphoreType.DMA((40,)),
             pltpu.SemaphoreType.DMA((40,)),
         ],

time: 28.2 us -> 27.1 us (0.961)
  Pallas kernels: 27.2 us -> 26.1 us
    pallas_call x1, Pallas kernels: 27.2 us -> 26.1 us  [per_device(): pl.pallas_call(kernel, out_shape=pltpu.VMEM((VEC, LEAF_DEV * LEAF), F32),...]
where the time goes in v3:
time: 27.1 us; the launch traced here: 26.9 us
  Pallas kernels  26.1 us (96%)
  local copies, waits for them, and re-layouts  0.8 us (3%)
    pallas_call x1, Pallas kernels, per_device(): pl.pallas_call(kernel, out_shape=pltpu.VMEM((VEC, LEAF_DEV * LEAF), F32),...  26.1 us
    unnamed x1, local copies, waits for them, and re-layouts  0.8 us

profile of v3, /device:TPU:1, one launch (start us, length us, event | category | flops | bytes accessed | tf_op | source)
XLA Modules:
  0.0 26.9 jit_solution(15464740592741990608)
XLA Ops:
  0.0 26.1 %shard_map.91 = f32[32,4096]{1,0:T(8,128)S(1)} custom-call(bf16[32,4096]{1,0:T(8,128)(2,1)} %vec_h.1, bf16[16,6,256,256]{3,2,1,0:T(8,128)(2,1)} %tiles_h.1, s32[6,16]{1,0:T(8,128)} %bitcast.5, bf16[16,64,256]{2,1,0:T(8,128)(2,1)} %basis_h.1, bf16[16,64,64]{2,1,0:T(8,128)(2,1)} %lt_h.1, bf16[16,24,64,64]{3,2,1,0:T(8,128)(2,1)} %far_h.1, s32[16,24]{1,0:T(8,128)} %list_h.1, ...), custom_call_target="tpu_custom_call" | custom-call | flops 600000000 | bytes 29000000 | tf_op jit(solution)/shard_map/pallas_call | solution.py:352
  26.2 0.8 %copy.11 = f32[32,4096]{1,0:T(8,128)} copy(f32[32,4096]{1,0:T(8,128)S(1)} %shard_map.91) | data formatting | bytes 1048576

commit v4 on v3

--- a/solution.py
+++ b/solution.py
@@ -126,8 +126,6 @@
     c_near_list = local(8, near_h, near_s)
     c_far_list = local(9, list_h, far_s)
     ALL = [c_vec, c_basis, c_lt, c_tt, c_tc, c_own, c_tiles, c_far, c_near_list, c_far_list]
-    for copy in ALL[:3]:
-        copy.start()
 
     gx_up = ((a + 1) % GX, b)
     gx_down = ((a + GX - 1) % GX, b)
@@ -136,8 +134,10 @@
     group_y = [(a, flip(b, i)) for i in range(1, GY)]
     group_x = [(flip(a, i), b) for i in range(1, GX)]
     barrier = pltpu.get_barrier_semaphore()
-    for partner in group_y + group_x:
+    for partner in group_y[::-1] + group_x[::-1]:
         pl.semaphore_signal(barrier, inc=1, device_id=partner, device_id_type=MESH)
+    for copy in ALL[:3]:
+        copy.start()
 
     def remote(n, source, target, partner):
         return pltpu.make_async_remote_copy(
@@ -227,6 +227,10 @@
     for m in range(LEAF_DEV):
         near_sum[m] = dot(vec[:, m * LEAF : (m + 1) * LEAF], tiles[m, 0], NT)
 
+    for copy in x_gy[:2]:
+        copy.wait_recv()
+    for copy in x_corner[:2]:
+        copy.start()
     chain = turned_whole(found_t, first[0])
     for t in (1, 2, 3):
         chain = apply([chain], [matrix(found_t, first[t])])
@@ -240,9 +244,9 @@
     for n in range(4):
         tops[n] = top_weights[n]
 
-    for copy in x_gy:
-        copy.wait_recv()
-    for copy in x_corner:
+    for copy in x_gy[2:]:
+        copy.wait_recv()
+    for copy in x_corner[2:]:
         copy.start()
     for slot in (0, 12):
         for z in range(4):

time: 27.1 us -> 26.8 us (0.989)
  Pallas kernels: 26.1 us -> 25.8 us
    pallas_call x1, Pallas kernels: 26.1 us -> 25.8 us  [per_device(): pl.pallas_call(kernel, out_shape=pltpu.VMEM((VEC, LEAF_DEV * LEAF), F32),...]
where the time goes in v4:
time: 26.8 us; the launch traced here: 26.6 us
  Pallas kernels  25.8 us (96%)
  local copies, waits for them, and re-layouts  0.8 us (3%)
    pallas_call x1, Pallas kernels, per_device(): pl.pallas_call(kernel, out_shape=pltpu.VMEM((VEC, LEAF_DEV * LEAF), F32),...  25.8 us
    unnamed x1, local copies, waits for them, and re-layouts  0.8 us

profile of v4, /device:TPU:1, one launch (start us, length us, event | category | flops | bytes accessed | tf_op | source)
XLA Modules:
  0.0 26.6 jit_solution(6115223631323389314)
XLA Ops:
  0.0 25.8 %shard_map.91 = f32[32,4096]{1,0:T(8,128)S(1)} custom-call(bf16[32,4096]{1,0:T(8,128)(2,1)} %vec_h.1, bf16[16,6,256,256]{3,2,1,0:T(8,128)(2,1)} %tiles_h.1, s32[6,16]{1,0:T(8,128)} %bitcast.5, bf16[16,64,256]{2,1,0:T(8,128)(2,1)} %basis_h.1, bf16[16,64,64]{2,1,0:T(8,128)(2,1)} %lt_h.1, bf16[16,24,64,64]{3,2,1,0:T(8,128)(2,1)} %far_h.1, s32[16,24]{1,0:T(8,128)} %list_h.1, ...), custom_call_target="tpu_custom_call" | custom-call | flops 600000000 | bytes 29000000 | tf_op jit(solution)/shard_map/pallas_call | solution.py:356
  25.8 0.8 %copy.11 = f32[32,4096]{1,0:T(8,128)} copy(f32[32,4096]{1,0:T(8,128)S(1)} %shard_map.91) | data formatting | bytes 1048576
